TPU v7x, 32 devices: a whole 2x2x4 slice. The times are simulated.
32 devices in a mesh: row: 4 (over y, core), col: 8 (over z, x).
Axes of the slice: x: 2, y: 2, z: 4, core: 2. Of those that a mesh axis runs over, the one named last changes fastest.
Arguments:
- trailing_adjoint: float32 [1536, 1536], P('row', 'col'), may hold values from -3 to 3, as said below
- panel: float32 [1536, 256], P(('row', 'col')), may hold values from -0.15625 to 0.15625
- panel_adjoint: float32 [1536, 256], P(('row', 'col')), may hold values from -6 to 6
- diag_factor: float32 [256, 256], replicated, may hold values from -1 to 2, as said below
- diag_adjoint: float32 [256, 256], P('row', 'col'), may hold values from -6 to 6
Outputs:
- off_adjoint: float32 [1536, 256], P(('row', 'col'))
- block_adjoint: float32 [256, 256], replicated
Inputs may be any that keep to these rules, and one draw needn't show every extreme that they name: `trailing_adjoint`: symmetric. `diag_factor`: lower triangular with diagonal entries from 1 to 2.
All inputs are finite; a program needn't handle non-finite values.
Results may differ from a plain program's by a relative error of at most 0.000071.
Values sent between devices are 32-bit elements; how exact they have to be, the bound alone decides.
A program may use at most 64 MiB of HBM per device.

v0:
```python
import functools

import jax
import jax.numpy as jnp
from jax import lax
from jax.experimental import pallas as pl
from jax.experimental.pallas import tpu as pltpu
from jax.sharding import PartitionSpec as P

MESH = pl.DeviceIdType.MESH
HIGHEST = lax.Precision.HIGHEST
CHUNK = 384


def split(x):
    high = x.astype(jnp.bfloat16)
    return high, (x - high.astype(jnp.float32)).astype(jnp.bfloat16)


def one(a, b):
    return jnp.dot(a, b, preferred_element_type=jnp.float32)


def dot_parts(a, b):
    return one(a[0], b[0]) + (one(a[0], b[1]) + one(a[1], b[0]))


def dot(a, b):
    return dot_parts(split(a), split(b))


def tdot(a, b):
    return dot(a.T, b)


def exact_dot(a, b):
    return jnp.dot(a, b, precision=HIGHEST, preferred_element_type=jnp.float32)


def iotas(shape):
    return (
        lax.broadcasted_iota(jnp.int32, shape, 0),
        lax.broadcasted_iota(jnp.int32, shape, 1),
    )


def inverse_pair(first, second):
    size = first.shape[0]
    i, j = iotas(first.shape)
    blocks, inverses = (first, second), []
    for block in blocks:
        diagonal = jnp.where(i == j, block, 0.0)
        down = 1.0 / jnp.sum(diagonal, axis=1, keepdims=True)
        across = 1.0 / jnp.sum(diagonal, axis=0, keepdims=True)
        pair = ((i >> 1) == (j >> 1)) & (i > j)
        inverses.append(
            jnp.where(i == j, jnp.broadcast_to(down, block.shape), 0.0)
            - jnp.where(pair, block, 0.0) * down * across
        )
    level = 1
    while (1 << level) < size:
        below = ((i >> (level + 1)) == (j >> (level + 1))) & ((i >> level) > (j >> level))
        halves = [dot(x, jnp.where(below, block, 0.0)) for x, block in zip(inverses, blocks)]
        inverses = [x - dot(half, x) for x, half in zip(inverses, halves)]
        level += 1
    return inverses


def wait_bytes(ref, semaphore):
    pltpu.make_async_copy(ref, ref, semaphore).wait()


def kernel(
    nrows, ncols, a_ref, p_ref, pa_ref, l_ref, d_ref, x_ref, k_ref,
    pbuf, tbuf, ubuf, sbuf, fsend, fbuf, wsend, wrecv, wfull, ebuf, linv, linv_t,
    send_p, recv_row, recv_col, send_t, recv_t, send_w, recv_w, send_g, recv_g, send_e, recv_e,
    send_s, recv_s, send_f, recv_f,
):
    row, col = lax.axis_index("row"), lax.axis_index("col")
    count = nrows * ncols
    me = row * ncols + col
    stretch, width = p_ref.shape
    half = width // 2

    barrier = pltpu.get_barrier_semaphore()

    def greet(k, carry):
        peer = lax.rem(me + k, count)
        pl.semaphore_signal(
            barrier, inc=1, device_id=(peer // ncols, lax.rem(peer, ncols)), device_id_type=MESH
        )
        return carry

    lax.fori_loop(1, count, greet, 0)

    i, j = iotas((d_ref.shape[0], width))
    placed = tdot(d_ref[...], jnp.where(j == i + col * d_ref.shape[0], 1.0, 0.0))
    drows = d_ref.shape[1]
    lrows = l_ref[pl.ds(pl.multiple_of(row * drows, drows), drows), :]
    wsend[...] = tdot(lrows, placed) - tdot(pa_ref[...], p_ref[...])
    pbuf[pl.ds(pl.multiple_of(col * stretch, stretch), stretch), :] = p_ref[...]

    pl.semaphore_wait(barrier, count - 1)

    shard = pl.ds(pl.multiple_of(col * stretch, stretch), stretch)
    fours = ncols // 2
    place_c, parity = col // 2, lax.rem(col, 2)
    neighbour = 2 * place_c + 1 - parity
    summer = (lax.rem(me, nrows), me // nrows)
    owner = nrows * col + row
    fixed = owner == me

    def to_row(k, carry):
        pltpu.make_async_remote_copy(
            src_ref=p_ref,
            dst_ref=pbuf.at[shard],
            send_sem=send_p,
            recv_sem=recv_row.at[k],
            device_id=(row, 2 * lax.rem(place_c + k, fours) + parity),
            device_id_type=MESH,
        ).start()
        return carry

    lax.fori_loop(1, fours, to_row, 0)
    pltpu.make_async_remote_copy(
        src_ref=p_ref, dst_ref=pbuf.at[shard], send_sem=send_p, recv_sem=recv_col,
        device_id=(row, neighbour), device_id_type=MESH,
    ).start()

    def hand_on(k, carry):
        origin = 2 * lax.rem(place_c + fours - k, fours) + parity
        arrived = pbuf.at[pl.ds(pl.multiple_of(origin * stretch, stretch), stretch)]
        wait_bytes(arrived, recv_row.at[k])
        pltpu.make_async_remote_copy(
            src_ref=arrived, dst_ref=arrived, send_sem=send_p, recv_sem=recv_col,
            device_id=(row, neighbour), device_id_type=MESH,
        ).start()
        return carry

    lax.fori_loop(1, fours, hand_on, 0)

    @pl.when(jnp.logical_not(fixed))
    def _():
        pltpu.make_async_remote_copy(
            src_ref=p_ref, dst_ref=sbuf, send_sem=send_s, recv_sem=recv_s,
            device_id=summer, device_id_type=MESH,
        ).start()

    @pl.when(fixed)
    def _():
        sbuf[...] = p_ref[...]

    wait_bytes(pbuf.at[pl.ds(0, fours * stretch)], recv_col)
    rows = a_ref.shape[1]
    tbuf[...] = dot(a_ref[:, :CHUNK], pbuf[:CHUNK, :])
    if rows > CHUNK:

        def add_chunk(k, carry):
            part = pl.ds(pl.multiple_of(k * CHUNK, CHUNK), CHUNK)
            tbuf[...] += dot(a_ref[:, part], pbuf[part, :])
            return carry

        lax.fori_loop(1, rows // CHUNK, add_chunk, 0)

    def to_summer(k, carry):
        q = lax.rem(row + k, nrows)
        pltpu.make_async_remote_copy(
            src_ref=tbuf.at[pl.ds(pl.multiple_of(q * stretch, stretch), stretch)],
            dst_ref=ubuf.at[k - 1],
            send_sem=send_t,
            recv_sem=recv_t,
            device_id=(q, col),
            device_id_type=MESH,
        ).start()
        return carry

    lax.fori_loop(1, nrows, to_summer, 0)
    low, high = inverse_pair(l_ref[:half, :half], l_ref[half:, half:])
    linv[:half, :half] = low
    linv[:half, half:] = jnp.zeros((half, half), jnp.float32)
    linv[half:, half:] = high
    linv[half:, :half] = -dot(high, dot(l_ref[half:, :half], low))

    linv_t[...] = linv[...].T

    wait_bytes(ubuf, recv_t)
    mine = pl.ds(pl.multiple_of(row * stretch, stretch), stretch)
    fsend[...] = tbuf[mine, :] + jnp.sum(ubuf[...], axis=0)

    @pl.when(jnp.logical_not(fixed))
    def _():
        wait_bytes(sbuf, recv_s)

    wsend[...] += 2.0 * tdot(fsend[...], sbuf[...])

    direct = count * 8 <= width
    group = count if direct else ncols
    place = me if direct else col
    piece = width // group

    def device_of(q):
        return (q // ncols, lax.rem(q, ncols)) if direct else (row, q)

    def scatter(k, carry):
        q = lax.rem(place + k, group)
        pltpu.make_async_remote_copy(
            src_ref=wsend.at[pl.ds(pl.multiple_of(q * piece, piece), piece)],
            dst_ref=wrecv.at[k - 1],
            send_sem=send_w,
            recv_sem=recv_w,
            device_id=device_of(q),
            device_id_type=MESH,
        ).start()
        return carry

    lax.fori_loop(1, group, scatter, 0)

    @pl.when(jnp.logical_not(fixed))
    def _():
        pltpu.make_async_remote_copy(
            src_ref=fsend, dst_ref=fbuf, send_sem=send_f, recv_sem=recv_f,
            device_id=(owner // ncols, lax.rem(owner, ncols)), device_id_type=MESH,
        ).start()

    @pl.when(fixed)
    def _():
        fbuf[...] = fsend[...]

    mine = pl.ds(pl.multiple_of(place * piece, piece), piece)
    wait_bytes(wrecv, recv_w)
    total = wsend[mine, :] + jnp.sum(wrecv[...], axis=0)
    if not direct:
        ebuf[row] = total

        def exchange(k, carry):
            pltpu.make_async_remote_copy(
                src_ref=ebuf.at[row],
                dst_ref=ebuf.at[row],
                send_sem=send_e,
                recv_sem=recv_e,
                device_id=(lax.rem(row + k, nrows), col),
                device_id_type=MESH,
            ).start()
            return carry

        lax.fori_loop(1, nrows, exchange, 0)
        wait_bytes(ebuf.at[pl.ds(0, nrows - 1)], recv_e)
        total = jnp.sum(ebuf[...], axis=0)
    wfull[mine, :] = total

    def gather(k, carry):
        pltpu.make_async_remote_copy(
            src_ref=wfull.at[mine],
            dst_ref=wfull.at[mine],
            send_sem=send_g,
            recv_sem=recv_g,
            device_id=device_of(lax.rem(place + k, group)),
            device_id_type=MESH,
        ).start()
        return carry

    lax.fori_loop(1, group, gather, 0)

    @pl.when(jnp.logical_not(fixed))
    def _():
        wait_bytes(fbuf, recv_f)

    x_ref[...] = dot(pa_ref[...] - 2.0 * fbuf[...], linv[...])

    wait_bytes(wfull.at[pl.ds(0, (group - 1) * piece)], recv_g)
    w = wfull[...]
    i, j = iotas(w.shape)
    lower = jnp.where(i > j, w, jnp.where(i == j, 0.5 * w, 0.0))
    symmetric = lower + lower.T
    inverse = split(linv[...])
    right = dot_parts(split(symmetric), inverse)
    k_ref[...] = 0.5 * dot_parts(split(linv_t[...]), split(right))

    wait_bytes(pbuf.at[pl.ds(0, (ncols - 1) * stretch)], send_p)
    wait_bytes(ubuf, send_t)

    @pl.when(jnp.logical_not(fixed))
    def _():
        wait_bytes(sbuf, send_s)
        wait_bytes(fbuf, send_f)

    wait_bytes(wrecv, send_w)
    wait_bytes(wfull.at[pl.ds(0, (group - 1) * piece)], send_g)
    if not direct:
        wait_bytes(ebuf.at[pl.ds(0, nrows - 1)], send_e)


def body(trailing_adjoint, panel, panel_adjoint, diag_factor, diag_adjoint):
    nrows, ncols = lax.axis_size("row"), lax.axis_size("col")
    stretch, width = panel.shape
    group = nrows * ncols if nrows * ncols * 8 <= width else ncols
    piece = width // group
    vmem = lambda *shape: pltpu.VMEM(shape, jnp.float32)
    return pl.pallas_call(
        functools.partial(kernel, nrows, ncols),
        out_shape=(
            jax.ShapeDtypeStruct(panel.shape, jnp.float32),
            jax.ShapeDtypeStruct(diag_factor.shape, jnp.float32),
        ),
        in_specs=[pl.BlockSpec(memory_space=pltpu.VMEM)] * 5,
        out_specs=(pl.BlockSpec(memory_space=pltpu.VMEM),) * 2,
        scratch_shapes=[
            vmem(ncols * stretch, width),
            vmem(nrows * stretch, width),
            vmem(nrows - 1, stretch, width),
            vmem(stretch, width),
            vmem(stretch, width),
            vmem(stretch, width),
            vmem(width, width),
            vmem(group - 1, piece, width),
            vmem(width, width),
            vmem(nrows, piece, width),
            vmem(width, width),
            vmem(width, width),
        ]
        + [pltpu.SemaphoreType.DMA, pltpu.SemaphoreType.DMA((ncols // 2,))]
        + [pltpu.SemaphoreType.DMA] * 13,
        compiler_params=pltpu.CompilerParams(
            collective_id=0, has_side_effects=True, vmem_limit_bytes=40 * 1024 * 1024
        ),
    )(trailing_adjoint.T, panel, panel_adjoint, diag_factor, diag_adjoint.T)


def solution(mesh):
    return jax.shard_map(
        body,
        mesh=mesh,
        in_specs=(
            P("row", "col"),
            P(("row", "col"), None),
            P(("row", "col"), None),
            P(),
            P("row", "col"),
        ),
        out_specs=(P(("row", "col"), None), P()),
        check_vma=False,
    )
```

profile of v0, /device:TPU:0, one launch (start us, length us, event | category | flops | bytes accessed | tf_op | source)
XLA Modules:
  0.0 44.4 jit_solution(9444551703876428168)
XLA Ops:
  0.6 0.0 copy-start
  0.6 1.0 %copy-done = f32[384,192]{0,1:T(8,128)S(1)} copy-done((f32[384,192]{0,1:T(8,128)S(1)}, f32[384,192]{0,1:T(8,128)}, u32[]{:S(2)}) %copy-start) | copy-done | bytes 294936
  1.6 0.0 copy-start.1
  1.6 0.9 %copy-done.1 = f32[256,256]{1,0:T(8,128)S(1)} copy-done((f32[256,256]{1,0:T(8,128)S(1)}, f32[256,256]{1,0:T(8,128)}, u32[]{:S(2)}) %copy-start.1) | copy-done | bytes 262168
  2.5 0.0 copy-start.2
  2.5 0.8 %copy-done.2 = f32[48,256]{1,0:T(8,128)S(1)} copy-done((f32[48,256]{1,0:T(8,128)S(1)}, f32[48,256]{1,0:T(8,128)}, u32[]{:S(2)}) %copy-start.2) | copy-done | bytes 49176
  3.3 0.0 copy-start.3
  3.3 0.8 %copy-done.3 = f32[48,256]{1,0:T(8,128)S(1)} copy-done((f32[48,256]{1,0:T(8,128)S(1)}, f32[48,256]{1,0:T(8,128)}, u32[]{:S(2)}) %copy-start.3) | copy-done | bytes 49176
  4.1 0.0 copy-start.4
  4.1 0.7 %copy-done.4 = f32[64,32]{0,1:T(8,128)S(1)} copy-done((f32[64,32]{0,1:T(8,128)S(1)}, f32[64,32]{0,1:T(8,128)}, u32[]{:S(2)}) %copy-start.4) | copy-done | bytes 8216
  4.9 38.2 %shard_map.68 = (f32[48,256]{1,0:T(8,128)S(1)}, f32[256,256]{1,0:T(8,128)S(1)}) custom-call(f32[192,384]{1,0:T(8,128)S(1)} %bitcast.2, f32[48,256]{1,0:T(8,128)S(1)} %copy-done.2, f32[48,256]{1,0:T(8,128)S(1)} %copy-done.3, f32[256,256]{1,0:T(8,128)S(1)} %copy-done.1, f32[32,64]{1,0:T(8,128)S(1)} %bitcast.3), custom_call_target="tpu_custom_call" | custom-call | tf_op jit(solution)/shard_map/pallas_call | solution.py:299
  43.1 0.6 %copy.9 = f32[48,256]{1,0:T(8,128)} copy(f32[48,256]{1,0:T(8,128)S(1)} %get-tuple-element.4) | data formatting | bytes 98304
  43.7 0.7 %copy.10 = f32[256,256]{1,0:T(8,128)} copy(f32[256,256]{1,0:T(8,128)S(1)} %get-tuple-element.5) | data formatting | bytes 524288
Async XLA Ops:
  0.6 1.0 %copy-start = (f32[384,192]{0,1:T(8,128)S(1)}, f32[384,192]{0,1:T(8,128)}, u32[]{:S(2)}) copy-start(f32[384,192]{0,1:T(8,128)} %param.5) | copy-start | bytes 884740
  1.6 0.9 %copy-start.1 = (f32[256,256]{1,0:T(8,128)S(1)}, f32[256,256]{1,0:T(8,128)}, u32[]{:S(2)}) copy-start(f32[256,256]{1,0:T(8,128)} %l_ref.1) | copy-start | bytes 786436
  2.5 0.8 %copy-start.2 = (f32[48,256]{1,0:T(8,128)S(1)}, f32[48,256]{1,0:T(8,128)}, u32[]{:S(2)}) copy-start(f32[48,256]{1,0:T(8,128)} %p_ref.1) | copy-start | bytes 147460
  3.3 0.8 %copy-start.3 = (f32[48,256]{1,0:T(8,128)S(1)}, f32[48,256]{1,0:T(8,128)}, u32[]{:S(2)}) copy-start(f32[48,256]{1,0:T(8,128)} %pa_ref.1) | copy-start | bytes 147460
  4.1 0.7 %copy-start.4 = (f32[64,32]{0,1:T(8,128)S(1)}, f32[64,32]{0,1:T(8,128)}, u32[]{:S(2)}) copy-start(f32[64,32]{0,1:T(8,128)} %param.9) | copy-start | bytes 24580
where the time goes:
time: 44.8 us; the launch traced here: 44.4 us
  Pallas kernels  38.2 us (85%)
  local copies, waits for them, and re-layouts  5.54 us (12%)
  between operations  0.65 us (1%)
    pallas_call x1, Pallas kernels, body(): pl.pallas_call(functools.partial(kernel, nrows, ncols), out_shape=(jax.Sh...  38.2 us
    unnamed x12, local copies, waits for them, and re-layouts  5.54 us

commit v1 on v0

--- a/solution.py
+++ b/solution.py
@@ -203,14 +203,20 @@
 
     def scatter(k, carry):
         q = lax.rem(place + k, group)
-        pltpu.make_async_remote_copy(
-            src_ref=wsend.at[pl.ds(pl.multiple_of(q * piece, piece), piece)],
-            dst_ref=wrecv.at[k - 1],
-            send_sem=send_w,
-            recv_sem=recv_w,
-            device_id=device_of(q),
-            device_id_type=MESH,
-        ).start()
+        part = pl.ds(pl.multiple_of(q * piece, piece), piece)
+
+        def send(columns):
+            pltpu.make_async_remote_copy(
+                src_ref=wsend.at[part, :columns],
+                dst_ref=wrecv.at[k - 1, :, :columns],
+                send_sem=send_w,
+                recv_sem=recv_w,
+                device_id=device_of(q),
+                device_id_type=MESH,
+            ).start()
+
+        pl.when(q < group // 2)(lambda: send(half))
+        pl.when(q >= group // 2)(lambda: send(width))
         return carry
 
     lax.fori_loop(1, group, scatter, 0)
@@ -227,7 +233,17 @@
         fbuf[...] = fsend[...]
 
     mine = pl.ds(pl.multiple_of(place * piece, piece), piece)
-    wait_bytes(wrecv, recv_w)
+    upper = place < group // 2
+
+    def others(semaphore):
+        rows = width + half
+        pl.when(upper)(lambda: wait_bytes(pbuf.at[: rows - piece, :half], semaphore))
+        pl.when(jnp.logical_not(upper))(
+            lambda: wait_bytes(pbuf.at[: rows - 2 * piece, :half], semaphore)
+        )
+
+    pl.when(upper)(lambda: wait_bytes(wrecv.at[:, :, :half], recv_w))
+    pl.when(jnp.logical_not(upper))(lambda: wait_bytes(wrecv, recv_w))
     total = wsend[mine, :] + jnp.sum(wrecv[...], axis=0)
     if not direct:
         ebuf[row] = total
@@ -249,14 +265,18 @@
     wfull[mine, :] = total
 
     def gather(k, carry):
-        pltpu.make_async_remote_copy(
-            src_ref=wfull.at[mine],
-            dst_ref=wfull.at[mine],
-            send_sem=send_g,
-            recv_sem=recv_g,
-            device_id=device_of(lax.rem(place + k, group)),
-            device_id_type=MESH,
-        ).start()
+        def send(columns):
+            pltpu.make_async_remote_copy(
+                src_ref=wfull.at[mine, :columns],
+                dst_ref=wfull.at[mine, :columns],
+                send_sem=send_g,
+                recv_sem=recv_g,
+                device_id=device_of(lax.rem(place + k, group)),
+                device_id_type=MESH,
+            ).start()
+
+        pl.when(upper)(lambda: send(half))
+        pl.when(jnp.logical_not(upper))(lambda: send(width))
         return carry
 
     lax.fori_loop(1, group, gather, 0)
@@ -267,7 +287,8 @@
 
     x_ref[...] = dot(pa_ref[...] - 2.0 * fbuf[...], linv[...])
 
-    wait_bytes(wfull.at[pl.ds(0, (group - 1) * piece)], recv_g)
+    others(recv_g)
+    wfull[:half, half:] = jnp.zeros((half, half), jnp.float32)
     w = wfull[...]
     i, j = iotas(w.shape)
     lower = jnp.where(i > j, w, jnp.where(i == j, 0.5 * w, 0.0))
@@ -284,8 +305,9 @@
         wait_bytes(sbuf, send_s)
         wait_bytes(fbuf, send_f)
 
-    wait_bytes(wrecv, send_w)
-    wait_bytes(wfull.at[pl.ds(0, (group - 1) * piece)], send_g)
+    others(send_w)
+    pl.when(upper)(lambda: wait_bytes(wrecv.at[:, :, :half], send_g))
+    pl.when(jnp.logical_not(upper))(lambda: wait_bytes(wrecv, send_g))
     if not direct:
         wait_bytes(ebuf.at[pl.ds(0, nrows - 1)], send_e)
 

time: 44.8 us -> 41.2 us (0.920)
  Pallas kernels: 38.2 us -> 34.7 us
    pallas_call x1, Pallas kernels: 38.2 us -> 34.7 us  [body(): pl.pallas_call(functools.partial(kernel, nrows, ncols), out_shape=(jax.Sh...]
where the time goes in v1:
time: 41.2 us; the launch traced here: 40.9 us
  Pallas kernels  34.7 us (84%)
  local copies, waits for them, and re-layouts  5.54 us (13%)
  between operations  0.65 us (2%)
    pallas_call x1, Pallas kernels, body(): pl.pallas_call(functools.partial(kernel, nrows, ncols), out_shape=(jax.Sh...  34.7 us
    unnamed x12, local copies, waits for them, and re-layouts  5.54 us

profile of v1, /device:TPU:0, one launch (start us, length us, event | category | flops | bytes accessed | tf_op | source)
XLA Modules:
  0.0 40.9 jit_solution(14103919537685188621)
XLA Ops:
  0.6 0.0 copy-start
  0.6 1.0 %copy-done = f32[384,192]{0,1:T(8,128)S(1)} copy-done((f32[384,192]{0,1:T(8,128)S(1)}, f32[384,192]{0,1:T(8,128)}, u32[]{:S(2)}) %copy-start) | copy-done | bytes 294936
  1.6 0.0 copy-start.1
  1.6 0.9 %copy-done.1 = f32[256,256]{1,0:T(8,128)S(1)} copy-done((f32[256,256]{1,0:T(8,128)S(1)}, f32[256,256]{1,0:T(8,128)}, u32[]{:S(2)}) %copy-start.1) | copy-done | bytes 262168
  2.5 0.0 copy-start.2
  2.5 0.8 %copy-done.2 = f32[48,256]{1,0:T(8,128)S(1)} copy-done((f32[48,256]{1,0:T(8,128)S(1)}, f32[48,256]{1,0:T(8,128)}, u32[]{:S(2)}) %copy-start.2) | copy-done | bytes 49176
  3.3 0.0 copy-start.3
  3.3 0.8 %copy-done.3 = f32[48,256]{1,0:T(8,128)S(1)} copy-done((f32[48,256]{1,0:T(8,128)S(1)}, f32[48,256]{1,0:T(8,128)}, u32[]{:S(2)}) %copy-start.3) | copy-done | bytes 49176
  4.1 0.0 copy-start.4
  4.1 0.7 %copy-done.4 = f32[64,32]{0,1:T(8,128)S(1)} copy-done((f32[64,32]{0,1:T(8,128)S(1)}, f32[64,32]{0,1:T(8,128)}, u32[]{:S(2)}) %copy-start.4) | copy-done | bytes 8216
  4.9 34.7 %shard_map.68 = (f32[48,256]{1,0:T(8,128)S(1)}, f32[256,256]{1,0:T(8,128)S(1)}) custom-call(f32[192,384]{1,0:T(8,128)S(1)} %bitcast.2, f32[48,256]{1,0:T(8,128)S(1)} %copy-done.2, f32[48,256]{1,0:T(8,128)S(1)} %copy-done.3, f32[256,256]{1,0:T(8,128)S(1)} %copy-done.1, f32[32,64]{1,0:T(8,128)S(1)} %bitcast.3), custom_call_target="tpu_custom_call" | custom-call | tf_op jit(solution)/shard_map/pallas_call | solution.py:321
  39.5 0.6 %copy.9 = f32[48,256]{1,0:T(8,128)} copy(f32[48,256]{1,0:T(8,128)S(1)} %get-tuple-element.4) | data formatting | bytes 98304
  40.2 0.7 %copy.10 = f32[256,256]{1,0:T(8,128)} copy(f32[256,256]{1,0:T(8,128)S(1)} %get-tuple-element.5) | data formatting | bytes 524288
Async XLA Ops:
  0.6 1.0 %copy-start = (f32[384,192]{0,1:T(8,128)S(1)}, f32[384,192]{0,1:T(8,128)}, u32[]{:S(2)}) copy-start(f32[384,192]{0,1:T(8,128)} %param.5) | copy-start | bytes 884740
  1.6 0.9 %copy-start.1 = (f32[256,256]{1,0:T(8,128)S(1)}, f32[256,256]{1,0:T(8,128)}, u32[]{:S(2)}) copy-start(f32[256,256]{1,0:T(8,128)} %l_ref.1) | copy-start | bytes 786436
  2.5 0.8 %copy-start.2 = (f32[48,256]{1,0:T(8,128)S(1)}, f32[48,256]{1,0:T(8,128)}, u32[]{:S(2)}) copy-start(f32[48,256]{1,0:T(8,128)} %p_ref.1) | copy-start | bytes 147460
  3.3 0.8 %copy-start.3 = (f32[48,256]{1,0:T(8,128)S(1)}, f32[48,256]{1,0:T(8,128)}, u32[]{:S(2)}) copy-start(f32[48,256]{1,0:T(8,128)} %pa_ref.1) | copy-start | bytes 147460
  4.1 0.7 %copy-start.4 = (f32[64,32]{0,1:T(8,128)S(1)}, f32[64,32]{0,1:T(8,128)}, u32[]{:S(2)}) copy-start(f32[64,32]{0,1:T(8,128)} %param.9) | copy-start | bytes 24580

commit v2 on v1

--- a/solution.py
+++ b/solution.py
@@ -264,6 +264,15 @@
         total = jnp.sum(ebuf[...], axis=0)
     wfull[mine, :] = total
 
+    paired = direct and nrows % 4 == 0
+    side, spread = lax.rem(row, 2), group // 2 if paired else group
+
+    def target(k):
+        if not paired:
+            return device_of(lax.rem(place + k, group))
+        q = lax.rem((row // 2) * ncols + col + k, spread)
+        return 2 * (q // ncols) + side, lax.rem(q, ncols)
+
     def gather(k, carry):
         def send(columns):
             pltpu.make_async_remote_copy(
@@ -271,7 +280,7 @@
                 dst_ref=wfull.at[mine, :columns],
                 send_sem=send_g,
                 recv_sem=recv_g,
-                device_id=device_of(lax.rem(place + k, group)),
+                device_id=target(k),
                 device_id_type=MESH,
             ).start()
 
@@ -279,7 +288,26 @@
         pl.when(jnp.logical_not(upper))(lambda: send(width))
         return carry
 
-    lax.fori_loop(1, group, gather, 0)
+    lax.fori_loop(1, spread, gather, 0)
+
+    if paired:
+        rows = 3 * width // 4
+        pl.when(upper)(lambda: wait_bytes(pbuf.at[: rows - piece, :half], recv_g))
+        pl.when(jnp.logical_not(upper))(
+            lambda: wait_bytes(pbuf.at[: rows - 2 * piece, :half], recv_g)
+        )
+        band = ncols * piece
+        for q in range(nrows // 2):
+            part = pl.ds(pl.multiple_of((2 * q + side) * band, band), band)
+            columns = half if q < nrows // 4 else width
+            pltpu.make_async_remote_copy(
+                src_ref=wfull.at[part, :columns],
+                dst_ref=wfull.at[part, :columns],
+                send_sem=send_e,
+                recv_sem=recv_e,
+                device_id=(row + 1 - 2 * side, col),
+                device_id_type=MESH,
+            ).start()
 
     @pl.when(jnp.logical_not(fixed))
     def _():
@@ -287,7 +315,10 @@
 
     x_ref[...] = dot(pa_ref[...] - 2.0 * fbuf[...], linv[...])
 
-    others(recv_g)
+    if paired:
+        wait_bytes(pbuf.at[: 3 * width // 4, :half], recv_e)
+    else:
+        others(recv_g)
     wfull[:half, half:] = jnp.zeros((half, half), jnp.float32)
     w = wfull[...]
     i, j = iotas(w.shape)
@@ -306,8 +337,10 @@
         wait_bytes(fbuf, send_f)
 
     others(send_w)
-    pl.when(upper)(lambda: wait_bytes(wrecv.at[:, :, :half], send_g))
-    pl.when(jnp.logical_not(upper))(lambda: wait_bytes(wrecv, send_g))
+    pl.when(upper)(lambda: wait_bytes(wrecv.at[: spread - 1, :, :half], send_g))
+    pl.when(jnp.logical_not(upper))(lambda: wait_bytes(wrecv.at[: spread - 1], send_g))
+    if paired:
+        wait_bytes(pbuf.at[: 3 * width // 4, :half], send_e)
     if not direct:
         wait_bytes(ebuf.at[pl.ds(0, nrows - 1)], send_e)
 

time: 41.2 us -> 41 us (level); the launches traced: 40.9 us -> 40.2 us
  Pallas kernels: 34.7 us -> 34 us
    pallas_call x1, Pallas kernels: 34.7 us -> 34 us  [body(): pl.pallas_call(functools.partial(kernel, nrows, ncols), out_shape=(jax.Sh...]
where the time goes in v2:
time: 41 us; the launch traced here: 40.2 us
  Pallas kernels  34 us (83%)
  local copies, waits for them, and re-layouts  5.54 us (14%)
  between operations  0.65 us (2%)
    pallas_call x1, Pallas kernels, body(): pl.pallas_call(functools.partial(kernel, nrows, ncols), out_shape=(jax.Sh...  34 us
    unnamed x12, local copies, waits for them, and re-layouts  5.54 us

profile of v2, /device:TPU:0, one launch (start us, length us, event | category | flops | bytes accessed | tf_op | source)
XLA Modules:
  0.0 40.2 jit_solution(14616576622805052449)
XLA Ops:
  0.6 0.0 copy-start
  0.6 1.0 %copy-done = f32[384,192]{0,1:T(8,128)S(1)} copy-done((f32[384,192]{0,1:T(8,128)S(1)}, f32[384,192]{0,1:T(8,128)}, u32[]{:S(2)}) %copy-start) | copy-done | bytes 294936
  1.6 0.0 copy-start.1
  1.6 0.9 %copy-done.1 = f32[256,256]{1,0:T(8,128)S(1)} copy-done((f32[256,256]{1,0:T(8,128)S(1)}, f32[256,256]{1,0:T(8,128)}, u32[]{:S(2)}) %copy-start.1) | copy-done | bytes 262168
  2.5 0.0 copy-start.2
  2.5 0.8 %copy-done.2 = f32[48,256]{1,0:T(8,128)S(1)} copy-done((f32[48,256]{1,0:T(8,128)S(1)}, f32[48,256]{1,0:T(8,128)}, u32[]{:S(2)}) %copy-start.2) | copy-done | bytes 49176
  3.3 0.0 copy-start.3
  3.3 0.8 %copy-done.3 = f32[48,256]{1,0:T(8,128)S(1)} copy-done((f32[48,256]{1,0:T(8,128)S(1)}, f32[48,256]{1,0:T(8,128)}, u32[]{:S(2)}) %copy-start.3) | copy-done | bytes 49176
  4.1 0.0 copy-start.4
  4.1 0.7 %copy-done.4 = f32[64,32]{0,1:T(8,128)S(1)} copy-done((f32[64,32]{0,1:T(8,128)S(1)}, f32[64,32]{0,1:T(8,128)}, u32[]{:S(2)}) %copy-start.4) | copy-done | bytes 8216
  4.9 34.0 %shard_map.68 = (f32[48,256]{1,0:T(8,128)S(1)}, f32[256,256]{1,0:T(8,128)S(1)}) custom-call(f32[192,384]{1,0:T(8,128)S(1)} %bitcast.2, f32[48,256]{1,0:T(8,128)S(1)} %copy-done.2, f32[48,256]{1,0:T(8,128)S(1)} %copy-done.3, f32[256,256]{1,0:T(8,128)S(1)} %copy-done.1, f32[32,64]{1,0:T(8,128)S(1)} %bitcast.3), custom_call_target="tpu_custom_call" | custom-call | tf_op jit(solution)/shard_map/pallas_call | solution.py:354
  38.9 0.6 %copy.9 = f32[48,256]{1,0:T(8,128)} copy(f32[48,256]{1,0:T(8,128)S(1)} %get-tuple-element.4) | data formatting | bytes 98304
  39.5 0.7 %copy.10 = f32[256,256]{1,0:T(8,128)} copy(f32[256,256]{1,0:T(8,128)S(1)} %get-tuple-element.5) | data formatting | bytes 524288
Async XLA Ops:
  0.6 1.0 %copy-start = (f32[384,192]{0,1:T(8,128)S(1)}, f32[384,192]{0,1:T(8,128)}, u32[]{:S(2)}) copy-start(f32[384,192]{0,1:T(8,128)} %param.5) | copy-start | bytes 884740
  1.6 0.9 %copy-start.1 = (f32[256,256]{1,0:T(8,128)S(1)}, f32[256,256]{1,0:T(8,128)}, u32[]{:S(2)}) copy-start(f32[256,256]{1,0:T(8,128)} %l_ref.1) | copy-start | bytes 786436
  2.5 0.8 %copy-start.2 = (f32[48,256]{1,0:T(8,128)S(1)}, f32[48,256]{1,0:T(8,128)}, u32[]{:S(2)}) copy-start(f32[48,256]{1,0:T(8,128)} %p_ref.1) | copy-start | bytes 147460
  3.3 0.8 %copy-start.3 = (f32[48,256]{1,0:T(8,128)S(1)}, f32[48,256]{1,0:T(8,128)}, u32[]{:S(2)}) copy-start(f32[48,256]{1,0:T(8,128)} %pa_ref.1) | copy-start | bytes 147460
  4.1 0.7 %copy-start.4 = (f32[64,32]{0,1:T(8,128)S(1)}, f32[64,32]{0,1:T(8,128)}, u32[]{:S(2)}) copy-start(f32[64,32]{0,1:T(8,128)} %param.9) | copy-start | bytes 24580

commit v3 on v2

--- a/solution.py
+++ b/solution.py
@@ -315,6 +315,7 @@
 
     x_ref[...] = dot(pa_ref[...] - 2.0 * fbuf[...], linv[...])
 
+    inverse, inverse_t = split(linv[...]), split(linv_t[...])
     if paired:
         wait_bytes(pbuf.at[: 3 * width // 4, :half], recv_e)
     else:
@@ -324,9 +325,8 @@
     i, j = iotas(w.shape)
     lower = jnp.where(i > j, w, jnp.where(i == j, 0.5 * w, 0.0))
     symmetric = lower + lower.T
-    inverse = split(linv[...])
     right = dot_parts(split(symmetric), inverse)
-    k_ref[...] = 0.5 * dot_parts(split(linv_t[...]), split(right))
+    k_ref[...] = 0.5 * dot_parts(inverse_t, split(right))
 
     wait_bytes(pbuf.at[pl.ds(0, (ncols - 1) * stretch)], send_p)
     wait_bytes(ubuf, send_t)

time: 41 us -> 41 us (level)
  no operation moved by 1% of the time
where the time goes in v3:
time: 41 us; the launch traced here: 40.2 us
  Pallas kernels  34 us (83%)
  local copies, waits for them, and re-layouts  5.54 us (14%)
  between operations  0.65 us (2%)
    pallas_call x1, Pallas kernels, body(): pl.pallas_call(functools.partial(kernel, nrows, ncols), out_shape=(jax.Sh...  34 us
    unnamed x12, local copies, waits for them, and re-layouts  5.54 us

profile of v3, /device:TPU:0, one launch (start us, length us, event | category | flops | bytes accessed | tf_op | source)
XLA Modules:
  0.0 40.2 jit_solution(15199978406120176423)
XLA Ops:
  0.6 0.0 copy-start
  0.6 1.0 %copy-done = f32[384,192]{0,1:T(8,128)S(1)} copy-done((f32[384,192]{0,1:T(8,128)S(1)}, f32[384,192]{0,1:T(8,128)}, u32[]{:S(2)}) %copy-start) | copy-done | bytes 294936
  1.6 0.0 copy-start.1
  1.6 0.9 %copy-done.1 = f32[256,256]{1,0:T(8,128)S(1)} copy-done((f32[256,256]{1,0:T(8,128)S(1)}, f32[256,256]{1,0:T(8,128)}, u32[]{:S(2)}) %copy-start.1) | copy-done | bytes 262168
  2.5 0.0 copy-start.2
  2.5 0.8 %copy-done.2 = f32[48,256]{1,0:T(8,128)S(1)} copy-done((f32[48,256]{1,0:T(8,128)S(1)}, f32[48,256]{1,0:T(8,128)}, u32[]{:S(2)}) %copy-start.2) | copy-done | bytes 49176
  3.3 0.0 copy-start.3
  3.3 0.8 %copy-done.3 = f32[48,256]{1,0:T(8,128)S(1)} copy-done((f32[48,256]{1,0:T(8,128)S(1)}, f32[48,256]{1,0:T(8,128)}, u32[]{:S(2)}) %copy-start.3) | copy-done | bytes 49176
  4.1 0.0 copy-start.4
  4.1 0.7 %copy-done.4 = f32[64,32]{0,1:T(8,128)S(1)} copy-done((f32[64,32]{0,1:T(8,128)S(1)}, f32[64,32]{0,1:T(8,128)}, u32[]{:S(2)}) %copy-start.4) | copy-done | bytes 8216
  4.9 34.0 %shard_map.68 = (f32[48,256]{1,0:T(8,128)S(1)}, f32[256,256]{1,0:T(8,128)S(1)}) custom-call(f32[192,384]{1,0:T(8,128)S(1)} %bitcast.2, f32[48,256]{1,0:T(8,128)S(1)} %copy-done.2, f32[48,256]{1,0:T(8,128)S(1)} %copy-done.3, f32[256,256]{1,0:T(8,128)S(1)} %copy-done.1, f32[32,64]{1,0:T(8,128)S(1)} %bitcast.3), custom_call_target="tpu_custom_call" | custom-call | tf_op jit(solution)/shard_map/pallas_call | solution.py:354
  38.9 0.6 %copy.9 = f32[48,256]{1,0:T(8,128)} copy(f32[48,256]{1,0:T(8,128)S(1)} %get-tuple-element.4) | data formatting | bytes 98304
  39.5 0.7 %copy.10 = f32[256,256]{1,0:T(8,128)} copy(f32[256,256]{1,0:T(8,128)S(1)} %get-tuple-element.5) | data formatting | bytes 524288
Async XLA Ops:
  0.6 1.0 %copy-start = (f32[384,192]{0,1:T(8,128)S(1)}, f32[384,192]{0,1:T(8,128)}, u32[]{:S(2)}) copy-start(f32[384,192]{0,1:T(8,128)} %param.5) | copy-start | bytes 884740
  1.6 0.9 %copy-start.1 = (f32[256,256]{1,0:T(8,128)S(1)}, f32[256,256]{1,0:T(8,128)}, u32[]{:S(2)}) copy-start(f32[256,256]{1,0:T(8,128)} %l_ref.1) | copy-start | bytes 786436
  2.5 0.8 %copy-start.2 = (f32[48,256]{1,0:T(8,128)S(1)}, f32[48,256]{1,0:T(8,128)}, u32[]{:S(2)}) copy-start(f32[48,256]{1,0:T(8,128)} %p_ref.1) | copy-start | bytes 147460
  3.3 0.8 %copy-start.3 = (f32[48,256]{1,0:T(8,128)S(1)}, f32[48,256]{1,0:T(8,128)}, u32[]{:S(2)}) copy-start(f32[48,256]{1,0:T(8,128)} %pa_ref.1) | copy-start | bytes 147460
  4.1 0.7 %copy-start.4 = (f32[64,32]{0,1:T(8,128)S(1)}, f32[64,32]{0,1:T(8,128)}, u32[]{:S(2)}) copy-start(f32[64,32]{0,1:T(8,128)} %param.9) | copy-start | bytes 24580
